TPU v7x, 256 devices: a whole 4x4x8 slice. The times are simulated.
256 devices in a mesh: dp: 32 (over x, y, core), vocab: 8 (over z).
Axes of the slice: x: 4, y: 4, z: 8, core: 2. Of those that a mesh axis runs over, the one named last changes fastest.
Arguments:
- student_hidden: bfloat16 [768, 3584], P('dp'), may hold values from -110 to 110
- teacher_hidden: bfloat16 [768, 4608], P('dp'), may hold values from -110 to 110
- student_head: bfloat16 [3584, 131072], P(None, ('dp', 'vocab')), may hold values from -0.09375 to 0.09375
- teacher_head: bfloat16 [4608, 131072], P(None, ('dp', 'vocab')), may hold values from -0.09375 to 0.09375
- live_count: int32 [32], P('dp'), may hold values from 1 to 24, as said below
- teacher_count: int32 [32], P('dp'), may hold values from 1 to 24, as said below
- teacher_dest: int32 [768], P('dp'), may hold values from 0 to 767, as said below
Outputs:
- distill_loss: float32 [], replicated
- grad_hidden: bfloat16 [768, 3584], P('dp', 'vocab')
- grad_head: bfloat16 [3584, 131072], P(None, ('dp', 'vocab'))
Inputs may be any that keep to these rules, and one draw needn't show every extreme that they name: Shard s's covered tokens are its first live_count[s] tokens; the counts sum to 384. Data shard j's filled teacher row slots are its first teacher_count[j] slots; the counts sum to 384. `teacher_dest`: A filled slot names the global index of a covered token; every covered token is named by exactly one filled slot. Unfilled slots hold arbitrary indices.
All inputs are finite; a program needn't handle non-finite values.
Results may differ from a plain program's by a relative error of at most 0.014.
Values may be sent and summed in bfloat16 or wider, within the bound.
No kernel may reach another device: no remote copies, remote signals or barrier semaphores. Data moves between devices by JAX's collectives and lax.ppermute only.
A program may use at most 128 MiB of HBM per device.

v0:
```python
import jax
import jax.numpy as jnp
from jax import lax
from jax.sharding import PartitionSpec as P

loss_scale = 65536.0


def per_device(
    student_hidden,
    teacher_hidden,
    student_head,
    teacher_head,
    live_count,
    teacher_count,
    teacher_dest,
):
    tok_dev = student_hidden.shape[0]
    data_size = lax.axis_size("dp")
    token_count = tok_dev * data_size
    live_total = token_count // 2
    grad_scale = loss_scale / live_total
    live_all, teach_all, dest_all = (
        lax.all_gather(live_count, "dp", axis=0, tiled=True),
        lax.all_gather(teacher_count, "dp", axis=0, tiled=True),
        lax.all_gather(teacher_dest, "dp", axis=0, tiled=True),
    )
    position = lax.broadcasted_iota(jnp.int32, (data_size, tok_dev), 1)
    live_flag = (position < live_all[:, None]).reshape(-1)
    slot_ok = (position < teach_all[:, None]).reshape(-1)
    gathered = lax.all_gather(student_hidden, "dp", axis=0, tiled=True)
    vocab_rows = student_head.shape[1]
    student_logits = jnp.dot(gathered, student_head, preferred_element_type=jnp.float32)
    packed = jnp.dot(
        lax.all_gather(teacher_hidden, "dp", axis=0, tiled=True),
        teacher_head,
        preferred_element_type=jnp.float32,
    )
    target = jnp.where(slot_ok, dest_all, token_count)
    teacher_logits = (
        jnp.zeros((token_count, vocab_rows), jnp.float32).at[target].set(packed, mode="drop")
    )
    teacher_top, student_top = lax.pmax(
        (jnp.max(teacher_logits, axis=1), jnp.max(student_logits, axis=1)), ("dp", "vocab")
    )
    teacher_weights = jnp.exp(teacher_logits - teacher_top[:, None])
    teacher_sum, student_sum, cross_sum = lax.psum(
        (
            jnp.sum(teacher_weights, axis=1),
            jnp.sum(jnp.exp(student_logits - student_top[:, None]), axis=1),
            jnp.sum(teacher_weights * (teacher_logits - student_logits), axis=1),
        ),
        ("dp", "vocab"),
    )
    teacher_norm = teacher_top + jnp.log(teacher_sum)
    student_norm = student_top + jnp.log(student_sum)
    divergence = cross_sum / teacher_sum - teacher_norm + student_norm
    distill_loss = jnp.sum(jnp.where(live_flag, divergence, 0.0)) / live_total
    probs_gap = jnp.exp(student_logits - student_norm[:, None]) - jnp.exp(
        teacher_logits - teacher_norm[:, None]
    )
    logit_grad = jnp.where(live_flag[:, None], probs_gap * grad_scale, 0.0).astype(jnp.bfloat16)
    grad_head = lax.dot_general(
        gathered, logit_grad, (((0,), (0,)), ((), ())), preferred_element_type=jnp.float32
    ).astype(jnp.bfloat16)
    columns = student_head.shape[0] // lax.axis_size("vocab")
    summed = lax.psum(
        lax.dot_general(
            logit_grad, student_head, (((1,), (1,)), ((), ())), preferred_element_type=jnp.float32
        ),
        ("dp", "vocab"),
    )
    own_block = lax.dynamic_slice(
        summed,
        (lax.axis_index("dp") * tok_dev, lax.axis_index("vocab") * columns),
        (tok_dev, columns),
    )
    return (distill_loss, own_block.astype(jnp.bfloat16), grad_head)


def solution(mesh):
    return jax.shard_map(
        per_device,
        mesh=mesh,
        in_specs=(
            P("dp", None),
            P("dp", None),
            P(None, ("dp", "vocab")),
            P(None, ("dp", "vocab")),
            P("dp"),
            P("dp"),
            P("dp"),
        ),
        out_specs=(P(), P("dp", "vocab"), P(None, ("dp", "vocab"))),
        check_vma=False,
    )
```

profile of v0, /device:TPU:1, one launch (start us, length us, event | category | flops | bytes accessed | tf_op | source)
XLA Modules:
  0.0 473.6 jit_solution(16044244641711408158)
XLA Ops:
  7.2 0.0 all-gather.5.cloned.1.call-start
  7.2 0.7 all-gather.5.cloned.1.call-update
  7.9 0.0 all-gather.3.cloned.1.call-start
  7.9 0.7 all-gather.3.cloned.1.call-update
  9.9 1.3 dynamic-slice
  11.9 0.8 dynamic-update-slice
  12.6 0.8 dynamic-update-slice.1
  13.4 0.8 dynamic-update-slice.2
  14.2 14.7 %all-reduce.3 = (s32[32]{0:T(128)S(1)}, s32[32]{0:T(128)S(1)}, s32[768]{0:T(1024)S(1)}) all-reduce(s32[32]{0:T(128)S(1)} %dynamic-update-slice, s32[32]{0:T(128)S(1)} %dynamic-update-slice.1, s32[768]{0:T(1024)S(1)} %dynamic-update-slice.2), channel_id=1, replica_groups=mesh['dp'=32,'vocab'=8] {'dp'}, use_global_device_ids=true, to_apply=%add | all-reduce | flops 832 | bytes 6656
  28.9 0.1 iota_compare_fusion.1
  29.0 0.1 lt.42
  29.1 0.1 iota_compare_fusion
  29.2 0.1 lt.45
  29.3 38.4 %all-gather.5.cloned.1.call-done = bf16[768,3584]{1,0:T(8,128)(2,1)} async-done(((bf16[24,3584]{1,0:T(8,128)(2,1)}), bf16[768,3584]{1,0:T(8,128)(2,1)}) %all-gather.5.cloned.1.call-update) | async-done | bytes 5505040 | tf_op jit(solution)/shard_map/all_gather | solution.py:31
  67.7 7.9 %fusion.4 = (f32[768]{0:T(1024)S(1)}, f32[768,512]{0,1:T(8,128)}) fusion(bf16[768,3584]{1,0:T(8,128)(2,1)} %all-gather.5.cloned.1.call-done, bf16[3584,512]{1,0:T(8,128)(2,1)} %param.9), kind=kOutput, calls=%fused_computation.17 | convolution fusion | flops 2818964736 | bytes 10750976 | tf_op jit(solution)/shard_map/dot_general | solution.py:33
  75.6 49.5 %all-gather.3.cloned.1.call-done = bf16[768,4608]{1,0:T(8,128)(2,1)} async-done(((bf16[24,4608]{1,0:T(8,128)(2,1)}), bf16[768,4608]{1,0:T(8,128)(2,1)}) %all-gather.3.cloned.1.call-update) | async-done | bytes 7077904 | tf_op jit(solution)/shard_map/all_gather | solution.py:35
  125.1 9.3 %fusion.5 = f32[768,512]{1,0:T(8,128)} fusion(bf16[768,4608]{1,0:T(8,128)(2,1)} %all-gather.3.cloned.1.call-done, bf16[4608,512]{1,0:T(8,128)(2,1)} %param.10), kind=kOutput, calls=%fused_computation.18 | convolution fusion | flops 3623878656 | bytes 13369344 | tf_op jit(solution)/shard_map/dot_general | solution.py:34
  134.4 6.6 %scatter_custom_fusion = f32[768,512]{1,0:T(8,128)S(1)} fusion(s32[768]{0:T(1024)S(1)} %compare_select_fusion, f32[768,512]{1,0:T(8,128)} %fusion.5, f32[]{:T(128)} %constant.12.clone.1), kind=kCustom, calls=%fused_computation.8 | custom fusion | bytes 1573376 | tf_op jit(solution)/shard_map/scatter | solution.py:41
  141.0 0.5 copy.12
  141.5 0.2 reduce_max.18
  141.6 75.6 %all-reduce.6 = (f32[768]{0:T(1024)S(1)}, f32[768]{0:T(1024)S(1)}) all-reduce(f32[768]{0:T(1024)S(1)} %get-tuple-element.21, f32[768]{0:T(1024)S(1)} %reduce_max.18), channel_id=1, replica_groups=mesh['dp'=32,'vocab'=8] {'dp','vocab'}, use_global_device_ids=true, to_apply=%region_8.9 | all-reduce | flops 1536 | bytes 12288 | tf_op jit(solution)/shard_map/pmax | solution.py:43
  217.3 2.1 multiply_reduce_fusion
  219.4 74.5 %all-reduce.5 = (f32[768]{0:T(1024)S(1)}, f32[768]{0:T(1024)S(1)}) all-reduce(f32[768]{0:T(1024)S(1)} %get-tuple-element.11, f32[768]{0:T(1024)S(1)} %get-tuple-element.10), channel_id=1, replica_groups=mesh['dp'=32,'vocab'=8] {'dp','vocab'}, use_global_device_ids=true, to_apply=%region_10.11 | all-reduce | flops 1536 | bytes 12288 | tf_op jit(solution)/shard_map/psum | solution.py:47
  293.9 0.0 slice-start
  293.9 0.5 select_convert_fusion
  294.4 0.0 slice-start.1
  294.4 8.2 %fusion.6 = f32[768,3584]{1,0:T(8,128)} fusion(bf16[768,512]{0,1:T(8,128)(2,1)S(1)} %select_convert_fusion, bf16[3584,512]{1,0:T(8,128)(2,1)} %param.9), kind=kOutput, calls=%fused_computation.19 | convolution fusion | flops 2818572288 | bytes 15466496 | tf_op jit(solution)/shard_map/dot_general | solution.py:68
  302.6 4.5 fusion
  307.1 5.9 %copy.15 = bf16[3584,512]{1,0:T(8,128)(2,1)} copy(bf16[3584,512]{0,1:T(8,128)(2,1)} %fusion) | data formatting | bytes 7340032
  313.0 149.9 %all-reduce.8 = (f32[768]{0:T(1024)S(1)}, bf16[768,3584]{1,0:T(8,128)(2,1)}) all-reduce(f32[768]{0:T(1024)S(1)} %get-tuple-element.9, f32[768,3584]{1,0:T(8,128)} %fusion.6), channel_id=1, replica_groups=mesh['dp'=32,'vocab'=8] {'dp','vocab'}, use_global_device_ids=true, to_apply=%region_4.5 | all-reduce | flops 2753280 | bytes 16521216 | tf_op jit(solution)/shard_map/psum | solution.py:47
  462.9 0.6 select_reduce_fusion
  464.2 1.5 dynamic_slice.5
  (10 shorter events, 0.0 us)
Async XLA Ops:
  7.2 60.5 %all-gather.5.cloned.1.call-start = ((), (), s32[]{:S(2)}) async-start(), calls=%async_computation.1 | async-start | bytes 5677056 | tf_op jit(solution)/shard_map/all_gather | solution.py:31
  7.9 117.2 %all-gather.3.cloned.1.call-start = ((), (), s32[]{:S(2)}) async-start(), calls=%async_computation | async-start | bytes 7299072 | tf_op jit(solution)/shard_map/all_gather | solution.py:35
  217.3 76.6 %copy-start = (f32[768,512]{0,1:T(8,128)S(1)}, f32[768,512]{0,1:T(8,128)}, u32[]{:S(2)}) copy-start(f32[768,512]{0,1:T(8,128)} %get-tuple-element.22) | copy-start | bytes 4718596
  293.9 8.7 %slice-start = ((s8[5505024]{0:T(1024)(128)(4,1)}), s8[4194304]{0:T(1024)(128)(4,1)S(1)}, s32[]{:S(2)}) async-start(s8[5505024]{0:T(1024)(128)(4,1)} %bitcast.13), calls=%async_computation.2 | async-start | bytes 8388608
  294.4 8.2 %slice-start.1 = ((s8[5505024]{0:T(1024)(128)(4,1)}), s8[1310720]{0:T(1024)(128)(4,1)S(1)}, s32[]{:S(2)}) async-start(s8[5505024]{0:T(1024)(128)(4,1)} %bitcast.13), calls=%async_computation.3 | async-start | bytes 2621440
Sparse Core Ops, SparseCore 0:
  10.5 57.1 all-gather.4
  70.2 54.7 all-gather.2
where the time goes:
time: 474 us
  blocking collectives  315 us (66%)
  waiting for transfers between devices  89.3 us (19%)
  matrix products  29.9 us (6%)
  local copies, waits for them, and re-layouts  18.2 us (4%)
  between operations  17.9 us (4%)
    psum x2, blocking collectives, per_device(): lax.psum((jnp.sum(teacher_weights, axis=1), jnp.sum(jnp.exp(student_logit...  224 us
    pmax x1, blocking collectives, per_device(): lax.pmax((jnp.max(teacher_logits, axis=1), jnp.max(student_logits, axis=1...  75.6 us
    all_gather x1, waiting for transfers between devices, per_device(): lax.all_gather(teacher_hidden, 'dp', axis=0, tiled=True)  49.5 us
    all_gather x1, waiting for transfers between devices, per_device(): gathered = lax.all_gather(student_hidden, 'dp', axis=0, tiled=True)  38.4 us
    unnamed x1, blocking collectives  14.7 us
    unnamed x14, local copies, waits for them, and re-layouts  9.54 us
  transfers between devices with their start and end apart: 2, of which 2 were waited for; matrix products, arithmetic and copies ran while one was open for 2% of the time, Pallas kernels for 0%

commit v1 on v0

--- a/solution.py
+++ b/solution.py
@@ -32,7 +32,9 @@
     vocab_rows = student_head.shape[1]
     student_logits = jnp.dot(gathered, student_head, preferred_element_type=jnp.float32)
     packed = jnp.dot(
-        lax.all_gather(teacher_hidden, "dp", axis=0, tiled=True),
+        jnp.concatenate(
+            lax.all_to_all(jnp.stack([teacher_hidden] * lax.axis_size("dp")), "dp", 0, 0), axis=0
+        ),
         teacher_head,
         preferred_element_type=jnp.float32,
     )

time: 474 us -> 490 us (1.034)
  blocking collectives: 315 us -> 409 us
  waiting for transfers between devices: 89.3 us -> 0.7 us
  starting transfers between devices: 0.08 us -> 8.81 us
    unnamed x1, blocking collectives: 14.7 us -> 96.4 us
    all_gather x1 -> x0, waiting for transfers between devices: 49.5 us -> none  [per_device(): lax.all_gather(teacher_hidden, 'dp', axis=0, tiled=True)]
    all_gather x1, waiting for transfers between devices: 38.4 us -> 0.02 us  [per_device(): gathered = lax.all_gather(student_hidden, 'dp', axis=0, tiled=True)]
    pmax x1, blocking collectives: 75.6 us -> 89.2 us  [per_device(): lax.pmax((jnp.max(teacher_logits, axis=1), jnp.max(student_logits, axis=1...]
    all_to_all x0 -> x1, starting transfers between devices: none -> 8.77 us  [per_device(): lax.all_to_all(jnp.stack([teacher_hidden] * lax.axis_size('dp')), 'dp', 0...]
  transfers between devices with their start and end apart: 2 -> 2, of which waited for: 2 -> 0; matrix products, arithmetic and copies ran while one was open for 2% -> 5% of each run, Pallas kernels for 0% -> 0%
where the time goes in v1:
time: 490 us; the launch traced here: 489 us
  blocking collectives  409 us (83%)
  matrix products  28.8 us (6%)
  local copies, waits for them, and re-layouts  21.3 us (4%)
  between operations  17.9 us (4%)
  starting transfers between devices  8.81 us (2%)
    psum x2, blocking collectives, per_device(): lax.psum((jnp.sum(teacher_weights, axis=1), jnp.sum(jnp.exp(student_logit...  224 us
    unnamed x1, blocking collectives  96.4 us
    pmax x1, blocking collectives, per_device(): lax.pmax((jnp.max(teacher_logits, axis=1), jnp.max(student_logits, axis=1...  89.2 us
  transfers between devices with their start and end apart: 2, of which 0 were waited for; matrix products, arithmetic and copies ran while one was open for 5% of the time, Pallas kernels for 0%

profile of v1, /device:TPU:1, one launch (start us, length us, event | category | flops | bytes accessed | tf_op | source)
XLA Modules:
  0.0 488.9 jit_solution(11512710569786858770)
XLA Ops:
  7.2 0.0 all-gather.2.cloned.1.call-start
  7.2 0.7 all-gather.2.cloned.1.call-update
  7.9 4.3 stack.2
  12.2 8.8 %all-to-all-start = ((bf16[32,24,4608]{2,1,0:T(8,128)(2,1)}), bf16[32,24,4608]{2,1,0:T(8,128)(2,1)}, u32[]{:S(2)}, u32[]{:S(2)}) async-start(bf16[32,24,4608]{2,1,0:T(8,128)(2,1)} %stack.2), calls=%async_computation | async-start | bytes 14155776 | tf_op jit(solution)/shard_map/all_to_all | solution.py:36
  22.3 0.6 dynamic-slice
  23.6 0.8 dynamic-update-slice
  24.3 0.8 dynamic-update-slice.1
  25.1 0.2 dynamic-update-slice.2
  25.3 96.4 %all-reduce.3 = (s32[32]{0:T(128)S(1)}, s32[32]{0:T(128)S(1)}, s32[768]{0:T(1024)S(1)}) all-reduce(s32[32]{0:T(128)S(1)} %dynamic-update-slice, s32[32]{0:T(128)S(1)} %dynamic-update-slice.1, s32[768]{0:T(1024)S(1)} %dynamic-update-slice.2), channel_id=1, replica_groups=mesh['dp'=32,'vocab'=8] {'dp'}, use_global_device_ids=true, to_apply=%add | all-reduce | flops 832 | bytes 6656
  121.7 0.1 iota_compare_fusion.1
  121.8 0.1 lt.42
  121.9 0.1 iota_compare_fusion
  122.0 0.1 lt.45
  122.1 0.0 all-to-all-done
  122.1 9.3 %fusion.5 = f32[768,512]{1,0:T(8,128)} fusion(bf16[768,4608]{1,0:T(8,128)(2,1)} %bitcast.2, bf16[4608,512]{1,0:T(8,128)(2,1)} %param.10), kind=kOutput, calls=%fused_computation.18 | convolution fusion | flops 3623878656 | bytes 13369344 | tf_op jit(solution)/shard_map/dot_general | solution.py:34
  131.4 6.6 %scatter_custom_fusion = f32[768,512]{1,0:T(8,128)S(1)} fusion(s32[768]{0:T(1024)S(1)} %compare_select_fusion, f32[768,512]{1,0:T(8,128)} %fusion.5, f32[]{:T(128)} %constant.12.clone.1), kind=kCustom, calls=%fused_computation.8 | custom fusion | bytes 1573376 | tf_op jit(solution)/shard_map/scatter | solution.py:43
  138.0 0.5 copy.12
  138.5 0.2 reduce_max.18
  138.7 0.0 all-gather.2.cloned.1.call-done
  138.7 6.8 %fusion.4 = (f32[768]{0:T(1024)S(1)}, f32[768,512]{0,1:T(8,128)S(1)}) fusion(bf16[768,3584]{1,0:T(8,128)(2,1)} %all-gather.2.cloned.1.call-done, bf16[3584,512]{1,0:T(8,128)(2,1)} %param.9), kind=kOutput, calls=%fused_computation.17 | convolution fusion | flops 2818964736 | bytes 10750976 | tf_op jit(solution)/shard_map/dot_general | solution.py:33
  145.5 89.2 %all-reduce.6 = (f32[768]{0:T(1024)S(1)}, f32[768]{0:T(1024)S(1)}) all-reduce(f32[768]{0:T(1024)S(1)} %get-tuple-element.21, f32[768]{0:T(1024)S(1)} %reduce_max.18), channel_id=1, replica_groups=mesh['dp'=32,'vocab'=8] {'dp','vocab'}, use_global_device_ids=true, to_apply=%region_8.9 | all-reduce | flops 1536 | bytes 12288 | tf_op jit(solution)/shard_map/pmax | solution.py:45
  234.7 0.6 multiply_reduce_fusion
  235.3 73.1 %all-reduce.5 = (f32[768]{0:T(1024)S(1)}, f32[768]{0:T(1024)S(1)}) all-reduce(f32[768]{0:T(1024)S(1)} %get-tuple-element.11, f32[768]{0:T(1024)S(1)} %get-tuple-element.10), channel_id=1, replica_groups=mesh['dp'=32,'vocab'=8] {'dp','vocab'}, use_global_device_ids=true, to_apply=%region_10.11 | all-reduce | flops 1536 | bytes 12288 | tf_op jit(solution)/shard_map/psum | solution.py:49
  308.4 0.5 select_convert_fusion
  308.9 0.0 slice-start.1
  308.9 8.1 %fusion.6 = f32[768,3584]{1,0:T(8,128)} fusion(bf16[768,512]{0,1:T(8,128)(2,1)S(1)} %select_convert_fusion, bf16[3584,512]{1,0:T(8,128)(2,1)} %param.9), kind=kOutput, calls=%fused_computation.19 | convolution fusion | flops 2818572288 | bytes 15466496 | tf_op jit(solution)/shard_map/dot_general | solution.py:70
  317.0 0.0 slice-done
  317.1 4.5 fusion
  321.6 5.9 %copy.15 = bf16[3584,512]{1,0:T(8,128)(2,1)} copy(bf16[3584,512]{0,1:T(8,128)(2,1)} %fusion) | data formatting | bytes 7340032
  327.5 150.7 %all-reduce.8 = (f32[768]{0:T(1024)S(1)}, bf16[768,3584]{1,0:T(8,128)(2,1)}) all-reduce(f32[768]{0:T(1024)S(1)} %get-tuple-element.9, f32[768,3584]{1,0:T(8,128)} %fusion.6), channel_id=1, replica_groups=mesh['dp'=32,'vocab'=8] {'dp','vocab'}, use_global_device_ids=true, to_apply=%region_4.5 | all-reduce | flops 2753280 | bytes 16521216 | tf_op jit(solution)/shard_map/psum | solution.py:49
  478.2 0.6 select_reduce_fusion
  479.4 1.5 dynamic_slice.5
  (12 shorter events, 0.0 us)
Async XLA Ops:
  7.2 131.5 %all-gather.2.cloned.1.call-start = ((), (), s32[]{:S(2)}) async-start(), calls=%async_computation.1 | async-start | bytes 5677056 | tf_op jit(solution)/shard_map/all_gather | solution.py:31
  12.2 10.1 %copy-start.1 = (u32[256]{0:T(256)S(1)}, u32[256]{0:T(256)}, u32[]{:S(2)}) copy-start(u32[256]{0:T(256)} %constant.38) | copy-start | bytes 3076
  12.2 12.9 %copy-start = (s32[24]{0:T(128)S(1)}, s32[24]{0:T(128)}, u32[]{:S(2)}) copy-start(s32[24]{0:T(128)} %param.13) | copy-start | bytes 292
  12.2 109.9 %all-to-all-start = ((bf16[32,24,4608]{2,1,0:T(8,128)(2,1)}), bf16[32,24,4608]{2,1,0:T(8,128)(2,1)}, u32[]{:S(2)}, u32[]{:S(2)}) async-start(bf16[32,24,4608]{2,1,0:T(8,128)(2,1)} %stack.2), calls=%async_computation | async-start | bytes 14155776 | tf_op jit(solution)/shard_map/all_to_all | solution.py:36
  308.4 8.7 %slice-start = ((s8[5505024]{0:T(1024)(128)(4,1)}), s8[4194304]{0:T(1024)(128)(4,1)S(1)}, s32[]{:S(2)}) async-start(s8[5505024]{0:T(1024)(128)(4,1)} %bitcast.14), calls=%async_computation.2 | async-start | bytes 8388608
  308.9 8.2 %slice-start.1 = ((s8[5505024]{0:T(1024)(128)(4,1)}), s8[1310720]{0:T(1024)(128)(4,1)S(1)}, s32[]{:S(2)}) async-start(s8[5505024]{0:T(1024)(128)(4,1)} %bitcast.14), calls=%async_computation.3 | async-start | bytes 2621440
Sparse Core Ops, SparseCore 0:
  10.5 113.9 all-gather.1
